TPU v7x, 32 devices: a whole 2x2x4 slice. The times are simulated.
32 devices in a mesh: dp: 8 (over z, y), expert: 4 (over x, core).
Axes of the slice: x: 2, y: 2, z: 4, core: 2. Of those that a mesh axis runs over, the one named last changes fastest.
Arguments:
- tokens: bfloat16 [4096, 2048], P(('dp', 'expert')), may hold values from -6 to 6
- routes: int32 [4096, 2], P(('dp', 'expert')), may hold values from 0 to 15, all different within a row; in each aligned block of 128 rows (0 to 127, 128 to 255, ...) at most 32 rows name the same one
- gate_codes: int32 [4096, 2], P(('dp', 'expert')), may hold values from 1 to 1024
- w_gate: bfloat16 [32, 2048, 384], P(('dp', 'expert')), may hold values from -0.125 to 0.125
- w_up: bfloat16 [32, 2048, 384], P(('dp', 'expert')), may hold values from -0.125 to 0.125
- w_down: bfloat16 [32, 384, 2048], P(('dp', 'expert')), may hold values from -0.21875 to 0.21875
- cot: bfloat16 [4096, 2048], P(('dp', 'expert')), may hold values from -6 to 6
Outputs:
- mixed: bfloat16 [4096, 2048], P(('dp', 'expert'))
- d_tokens: bfloat16 [4096, 2048], P(('dp', 'expert'))
- d_gate: bfloat16 [32, 2048, 384], P(('dp', 'expert'))
- d_up: bfloat16 [32, 2048, 384], P(('dp', 'expert'))
- d_down: bfloat16 [32, 384, 2048], P(('dp', 'expert'))
Inputs may be any that keep to these rules, and one draw needn't show every extreme that they name: `routes`: each row names 2 different experts; among the 128 rows of one device no expert is named more than 32 times, a bound that some block reaches. `gate_codes`: the gate weight is the value divided by 1024.
All inputs are finite; a program needn't handle non-finite values.
Results may differ from a plain program's by a relative error of at most 0.012.
Values may be sent and summed in bfloat16 or wider, within the bound.
A program may use at most 128 MiB of HBM per device.

v0:
```python
import jax
import jax.numpy as jnp
from jax import lax
from jax.sharding import PartitionSpec as P


def expert_work(xrows, qrows, w_gate, w_up, w_down):
    act = jnp.dot(xrows, w_gate, preferred_element_type=jnp.float32)
    upv = jnp.dot(xrows, w_up, preferred_element_type=jnp.float32)
    sig = jax.nn.sigmoid(act)
    silu = act * sig
    hidden = (silu * upv).astype(jnp.bfloat16)
    outv = jnp.dot(hidden, w_down, preferred_element_type=jnp.float32).astype(jnp.bfloat16)
    dhid = jnp.dot(qrows, w_down.T, preferred_element_type=jnp.float32)
    dact = (dhid * upv * sig * (1.0 + act * (1.0 - sig))).astype(jnp.bfloat16)
    dupv = (dhid * silu).astype(jnp.bfloat16)
    pgrad = (
        jnp.dot(dact, w_gate.T, preferred_element_type=jnp.float32)
        + jnp.dot(dupv, w_up.T, preferred_element_type=jnp.float32)
    ).astype(jnp.bfloat16)
    grad_g = jnp.dot(xrows.T, dact, preferred_element_type=jnp.float32).astype(jnp.bfloat16)
    grad_u = jnp.dot(xrows.T, dupv, preferred_element_type=jnp.float32).astype(jnp.bfloat16)
    grad_d = jnp.dot(hidden.T, qrows, preferred_element_type=jnp.float32).astype(jnp.bfloat16)
    return (outv, pgrad, grad_g, grad_u, grad_d)


def reorder(index, n_data, n_group, slots):
    device = index // slots
    within = index % slots
    return (device % n_group * n_data + device // n_group) * slots + within


def group_major(row_pair, n_data, n_group, slots):
    return row_pair.reshape(n_data, n_group, slots).transpose(1, 0, 2).reshape(-1)


def local(tokens, routes, gate_codes, w_gate, w_up, w_down, cot):
    tok_rows, top = routes.shape
    width = tokens.shape[1]
    n_data = lax.axis_size("dp")
    n_group = lax.axis_size("expert")
    devices = n_data * n_group
    experts = devices // 2
    most = max(2, 2 * tok_rows * top // experts)
    pairs = tok_rows * top
    expert_ids = routes.reshape(pairs)
    onehot = (expert_ids[:, None] == jnp.arange(experts, dtype=jnp.int32)[None, :]).astype(
        jnp.int32
    )
    before = jnp.cumsum(onehot, axis=0) - onehot
    position = jnp.sum(before * onehot, axis=1)
    gates = gate_codes.reshape(pairs).astype(jnp.float32) / 1024.0
    qpairs = (
        (gates.reshape(tok_rows, top, 1) * cot.astype(jnp.float32)[:, None, :])
        .astype(jnp.bfloat16)
        .reshape(pairs, width)
    )
    tok_pad = jnp.concatenate([tokens, jnp.zeros((1, width), jnp.bfloat16)], axis=0)
    q_pad = jnp.concatenate([qpairs, jnp.zeros((1, width), jnp.bfloat16)], axis=0)
    pair_ids = jnp.arange(pairs, dtype=jnp.int32)
    wg = w_gate[0]
    wu = w_up[0]
    wd = w_down[0]
    total = devices * most
    halves = jnp.arange(2, dtype=jnp.int32)
    targets = (2 * expert_ids[:, None] + halves[None, :]) * most + position[:, None]
    row_pair = (
        jnp.full((total,), pairs, jnp.int32).at[targets.reshape(-1)].set(jnp.repeat(pair_ids, 2))
    )
    row_pair = group_major(row_pair, n_data, n_group, most)
    row_token = jnp.where(row_pair < pairs, row_pair // top, tok_rows)
    xsend = tok_pad[row_token].reshape(n_group, n_data, most * width)
    qsend = q_pad[row_pair].reshape(n_group, n_data, most * width)
    xrecv, qrecv = (
        lax.all_to_all(
            lax.all_to_all(xsend, "dp", split_axis=1, concat_axis=1, tiled=True),
            "expert",
            split_axis=0,
            concat_axis=0,
            tiled=True,
        ),
        lax.all_to_all(
            lax.all_to_all(qsend, "dp", split_axis=1, concat_axis=1, tiled=True),
            "expert",
            split_axis=0,
            concat_axis=0,
            tiled=True,
        ),
    )
    outv, pgrad, grad_g, grad_u, grad_d = expert_work(
        xrecv.reshape(total, width), qrecv.reshape(total, width), wg, wu, wd
    )
    oback, pback = (
        lax.all_to_all(
            lax.all_to_all(
                outv.reshape(n_group, n_data, most * width),
                "dp",
                split_axis=1,
                concat_axis=1,
                tiled=True,
            ),
            "expert",
            split_axis=0,
            concat_axis=0,
            tiled=True,
        ),
        lax.all_to_all(
            lax.all_to_all(
                pgrad.reshape(n_group, n_data, most * width),
                "dp",
                split_axis=1,
                concat_axis=1,
                tiled=True,
            ),
            "expert",
            split_axis=0,
            concat_axis=0,
            tiled=True,
        ),
    )
    back_idx = reorder(targets, n_data, n_group, most)
    pair_out = jnp.sum(oback.reshape(total, width)[back_idx].astype(jnp.float32), axis=1)
    pair_grad = jnp.sum(pback.reshape(total, width)[back_idx].astype(jnp.float32), axis=1)
    mixed = jnp.sum((gates[:, None] * pair_out).reshape(tok_rows, top, width), axis=1).astype(
        jnp.bfloat16
    )
    d_tokens = jnp.sum(pair_grad.reshape(tok_rows, top, width), axis=1).astype(jnp.bfloat16)
    return (mixed, d_tokens, grad_g[None], grad_u[None], grad_d[None])


def solution(mesh):
    placed = (
        P(("dp", "expert"), None),
        P(("dp", "expert"), None),
        P(("dp", "expert"), None),
        P(("dp", "expert"), None, None),
        P(("dp", "expert"), None, None),
        P(("dp", "expert"), None, None),
        P(("dp", "expert"), None),
    )
    return jax.shard_map(
        local,
        mesh=mesh,
        in_specs=placed,
        out_specs=(
            P(("dp", "expert"), None),
            P(("dp", "expert"), None),
            P(("dp", "expert"), None, None),
            P(("dp", "expert"), None, None),
            P(("dp", "expert"), None, None),
        ),
        check_vma=False,
    )
```

profile of v0, /device:TPU:12, one launch (start us, length us, event | category | flops | bytes accessed | tf_op | source)
XLA Modules:
  0.0 697.3 jit_solution(15704112383791347527)
XLA Ops:
  0.6 0.9 copy.78
  1.7 0.1 eq.29
  1.9 0.6 reduce-window.6
  2.4 0.2 slice_reduce_fusion
  2.9 0.1 add.201
  3.2 2.4 scatter_custom_fusion
  5.9 1.1 concatenate.6
  7.0 6.1 gather_fusion
  13.0 5.6 reshape.463
  18.7 7.4 %copy.82 = bf16[4,8,65536]{2,0,1:T(4,128)(2,1)} copy(bf16[4,8,65536]{2,1,0:T(8,128)(2,1)} %reshape.463) | data formatting | bytes 8388608 | tf_op jit(solution)/shard_map/reshape | solution.py:72
  26.1 6.6 all-to-all-start
  33.0 2.4 mul.120
  35.4 3.7 mul.121
  39.0 1.8 multiply_convert_fusion
  40.9 6.0 gather_fusion.2
  47.0 5.6 reshape.467
  52.6 7.4 %copy.88 = bf16[4,8,65536]{2,0,1:T(4,128)(2,1)} copy(bf16[4,8,65536]{2,1,0:T(8,128)(2,1)} %reshape.467) | data formatting | bytes 8388608 | tf_op jit(solution)/shard_map/reshape | solution.py:73
  60.0 62.6 %all-to-all-done = bf16[4,8,65536]{2,0,1:T(4,128)(2,1)} async-done(((bf16[4,8,65536]{2,0,1:T(4,128)(2,1)}), bf16[4,8,65536]{2,0,1:T(4,128)(2,1)}, u32[]{:S(2)}, u32[]{:S(2)}) %all-to-all-start) | async-done | bytes 4194336 | tf_op jit(solution)/shard_map/all_to_all | solution.py:76
  122.5 7.8 %all-to-all-start.4 = ((bf16[4,8,65536]{2,0,1:T(4,128)(2,1)}), bf16[4,8,65536]{2,0,1:T(4,128)(2,1)}, u32[]{:S(2)}, u32[]{:S(2)}) async-start(bf16[4,8,65536]{2,0,1:T(4,128)(2,1)} %copy.88), calls=%async_computation.4 | async-start | bytes 8388608 | tf_op jit(solution)/shard_map/all_to_all | solution.py:83
  130.4 6.4 copy.83
  136.8 82.8 %all-to-all-done.4 = bf16[4,8,65536]{2,0,1:T(4,128)(2,1)} async-done(((bf16[4,8,65536]{2,0,1:T(4,128)(2,1)}), bf16[4,8,65536]{2,0,1:T(4,128)(2,1)}, u32[]{:S(2)}, u32[]{:S(2)}) %all-to-all-start.4) | async-done | bytes 4194336 | tf_op jit(solution)/shard_map/all_to_all | solution.py:83
  219.6 4.8 all-to-all-start.1
  224.5 6.4 copy.89
  230.9 41.8 %all-to-all-done.1 = bf16[4,8,65536]{2,1,0:T(8,128)(2,1)} async-done(((bf16[4,8,65536]{2,1,0:T(8,128)(2,1)}), bf16[4,8,65536]{2,1,0:T(8,128)(2,1)}, u32[]{:S(2)}, u32[]{:S(2)}) %all-to-all-start.1) | async-done | bytes 4194336 | tf_op jit(solution)/shard_map/all_to_all | solution.py:75
  272.7 5.1 all-to-all-start.5
  277.8 5.6 reshape.464
  283.5 6.3 fusion.7
  289.8 3.5 fusion.11
  293.2 32.8 %all-to-all-done.5 = bf16[4,8,65536]{2,1,0:T(8,128)(2,1)} async-done(((bf16[4,8,65536]{2,1,0:T(8,128)(2,1)}), bf16[4,8,65536]{2,1,0:T(8,128)(2,1)}, u32[]{:S(2)}, u32[]{:S(2)}) %all-to-all-start.5) | async-done | bytes 4194336 | tf_op jit(solution)/shard_map/all_to_all | solution.py:82
  326.0 5.7 reshape.468
  331.7 7.1 %multiply_convert_fusion.1 = (bf16[1024,384]{1,0:T(8,128)(2,1)}, bf16[1024,384]{1,0:T(8,128)(2,1)}, bf16[1024,384]{1,0:T(8,128)(2,1)S(1)}) fusion(f32[1024,384]{1,0:T(8,128)} %fusion.11, f32[1024,384]{1,0:T(8,128)} %fusion.7, bf16[1024,2048]{1,0:T(8,128)(2,1)} %reshape.468, bf16[1,384,2048]{2,1,0:T(8,128)(2,1)S(1)} %copy-done), kind=kOutput, calls=%fused_computation.25 | convolution fusion | flops 1616510976 | bytes 11272192 | tf_op jit(solution)/shard_map/dot_general | solution.py:14
  338.8 0.9 copy-done.11
  339.7 4.3 convolution_convert_fusion
  344.0 5.6 reshape.465
  349.6 7.4 %copy.84 = bf16[4,8,65536]{2,0,1:T(4,128)(2,1)} copy(bf16[4,8,65536]{2,1,0:T(8,128)(2,1)} %reshape.465) | data formatting | bytes 8388608 | tf_op jit(solution)/shard_map/reshape | solution.py:96
  357.0 8.3 %all-to-all-start.2 = ((bf16[4,8,65536]{2,0,1:T(4,128)(2,1)}), bf16[4,8,65536]{2,0,1:T(4,128)(2,1)}, u32[]{:S(2)}, u32[]{:S(2)}) async-start(bf16[4,8,65536]{2,0,1:T(4,128)(2,1)} %copy.84), calls=%async_computation.2 | async-start | bytes 8388608 | tf_op jit(solution)/shard_map/all_to_all | solution.py:95
  365.4 3.7 fusion.9
  369.0 4.3 add_convert_fusion
  373.4 5.7 reshape.469
  379.0 7.4 %copy.90 = bf16[4,8,65536]{2,0,1:T(4,128)(2,1)} copy(bf16[4,8,65536]{2,1,0:T(8,128)(2,1)} %reshape.469) | data formatting | bytes 8388608 | tf_op jit(solution)/shard_map/reshape | solution.py:109
  386.4 68.9 %all-to-all-done.2 = bf16[4,8,65536]{2,0,1:T(4,128)(2,1)} async-done(((bf16[4,8,65536]{2,0,1:T(4,128)(2,1)}), bf16[4,8,65536]{2,0,1:T(4,128)(2,1)}, u32[]{:S(2)}, u32[]{:S(2)}) %all-to-all-start.2) | async-done | bytes 4194336 | tf_op jit(solution)/shard_map/all_to_all | solution.py:95
  455.3 7.9 %all-to-all-start.6 = ((bf16[4,8,65536]{2,0,1:T(4,128)(2,1)}), bf16[4,8,65536]{2,0,1:T(4,128)(2,1)}, u32[]{:S(2)}, u32[]{:S(2)}) async-start(bf16[4,8,65536]{2,0,1:T(4,128)(2,1)} %copy.90), calls=%async_computation.6 | async-start | bytes 8388608 | tf_op jit(solution)/shard_map/all_to_all | solution.py:108
  463.1 6.5 copy.85
  469.6 82.8 %all-to-all-done.6 = bf16[4,8,65536]{2,0,1:T(4,128)(2,1)} async-done(((bf16[4,8,65536]{2,0,1:T(4,128)(2,1)}), bf16[4,8,65536]{2,0,1:T(4,128)(2,1)}, u32[]{:S(2)}, u32[]{:S(2)}) %all-to-all-start.6) | async-done | bytes 4194336 | tf_op jit(solution)/shard_map/all_to_all | solution.py:108
  552.4 5.0 all-to-all-start.3
  557.4 6.4 copy.91
  563.8 41.8 %all-to-all-done.3 = bf16[4,8,65536]{2,1,0:T(8,128)(2,1)} async-done(((bf16[4,8,65536]{2,1,0:T(8,128)(2,1)}), bf16[4,8,65536]{2,1,0:T(8,128)(2,1)}, u32[]{:S(2)}, u32[]{:S(2)}) %all-to-all-start.3) | async-done | bytes 4194336 | tf_op jit(solution)/shard_map/all_to_all | solution.py:94
  605.6 4.9 all-to-all-start.7
  610.5 0.3 compare_select_fusion
  611.0 5.3 fusion.2
  616.4 3.6 fusion.1
  619.9 3.6 fusion
  623.5 5.6 reshape.466
  629.2 8.0 %gather_fusion.1 = bf16[512,2048]{1,0:T(8,128)(2,1)} fusion(bf16[1024,2048]{1,0:T(8,128)(2,1)} %reshape.466, s32[1024]{0:T(1024)S(1)} %pad_clamp_fusion), kind=kCustom, calls=%fused_computation.1 | custom fusion | bytes 4196352 | tf_op jit(solution)/shard_map/gather | solution.py:122
  637.2 5.6 reshape.514
  642.8 8.5 %reduce_sum.48 = f32[256,2048]{1,0:T(8,128)} reduce(f32[256,2,2048]{2,1,0:T(2,128)} %reshape.514, f32[]{:T(128)} %constant.89.clone.1), dimensions={1}, to_apply=%region_4.5 | reduce | flops 524288 | bytes 6291460 | tf_op jit(solution)/shard_map/reduce_sum | solution.py:122
  651.3 3.5 reduce_sum.49
  654.8 5.6 multiply_reduce_fusion
  660.4 5.6 reshape.470
  666.0 8.2 %gather_fusion.3 = bf16[512,2048]{1,0:T(8,128)(2,1)} fusion(bf16[1024,2048]{1,0:T(8,128)(2,1)} %reshape.470, s32[1024]{0:T(1024)S(1)} %pad_clamp_fusion), kind=kCustom, calls=%fused_computation.3 | custom fusion | bytes 4196352 | tf_op jit(solution)/shard_map/gather | solution.py:123
  674.3 5.4 reshape.515
  679.7 8.5 %reduce_sum.51 = f32[256,2048]{1,0:T(8,128)} reduce(f32[256,2,2048]{2,1,0:T(2,128)} %reshape.515, f32[]{:T(128)} %constant.89.clone.1), dimensions={1}, to_apply=%region_6.7 | reduce | flops 524288 | bytes 6291460 | tf_op jit(solution)/shard_map/reduce_sum | solution.py:123
  688.2 3.6 reshape.471
  691.8 5.0 reduce_sum.52
  (48 shorter events, 1.4 us)
Async XLA Ops:
  0.6 331.1 %copy-start = (bf16[1,384,2048]{2,1,0:T(8,128)(2,1)S(1)}, bf16[1,384,2048]{2,1,0:T(8,128)(2,1)}, u32[]{:S(2)}) copy-start(bf16[1,384,2048]{2,1,0:T(8,128)(2,1)} %param.12) | copy-start | bytes 4718596
  26.1 6.6 copy-start.10
  26.1 6.9 copy-start.9
  26.1 96.4 %all-to-all-start = ((bf16[4,8,65536]{2,0,1:T(4,128)(2,1)}), bf16[4,8,65536]{2,0,1:T(4,128)(2,1)}, u32[]{:S(2)}, u32[]{:S(2)}) async-start(bf16[4,8,65536]{2,0,1:T(4,128)(2,1)} %copy.82), calls=%async_computation | async-start | bytes 8388608 | tf_op jit(solution)/shard_map/all_to_all | solution.py:76
  122.5 97.1 %all-to-all-start.4 = ((bf16[4,8,65536]{2,0,1:T(4,128)(2,1)}), bf16[4,8,65536]{2,0,1:T(4,128)(2,1)}, u32[]{:S(2)}, u32[]{:S(2)}) async-start(bf16[4,8,65536]{2,0,1:T(4,128)(2,1)} %copy.88), calls=%async_computation.4 | async-start | bytes 8388608 | tf_op jit(solution)/shard_map/all_to_all | solution.py:83
  219.6 53.1 %all-to-all-start.1 = ((bf16[4,8,65536]{2,1,0:T(8,128)(2,1)}), bf16[4,8,65536]{2,1,0:T(8,128)(2,1)}, u32[]{:S(2)}, u32[]{:S(2)}) async-start(bf16[4,8,65536]{2,1,0:T(8,128)(2,1)} %copy.83), calls=%async_computation.1 | async-start | bytes 8388608 | tf_op jit(solution)/shard_map/all_to_all | solution.py:75
  272.7 53.3 %all-to-all-start.5 = ((bf16[4,8,65536]{2,1,0:T(8,128)(2,1)}), bf16[4,8,65536]{2,1,0:T(8,128)(2,1)}, u32[]{:S(2)}, u32[]{:S(2)}) async-start(bf16[4,8,65536]{2,1,0:T(8,128)(2,1)} %copy.89), calls=%async_computation.5 | async-start | bytes 8388608 | tf_op jit(solution)/shard_map/all_to_all | solution.py:82
  283.5 6.3 copy-start.2
  283.5 6.3 copy-start.4
  338.8 0.9 copy-start.11
  357.0 98.2 %all-to-all-start.2 = ((bf16[4,8,65536]{2,0,1:T(4,128)(2,1)}), bf16[4,8,65536]{2,0,1:T(4,128)(2,1)}, u32[]{:S(2)}, u32[]{:S(2)}) async-start(bf16[4,8,65536]{2,0,1:T(4,128)(2,1)} %copy.84), calls=%async_computation.2 | async-start | bytes 8388608 | tf_op jit(solution)/shard_map/all_to_all | solution.py:95
  365.3 3.7 copy-start.5
  365.4 3.7 copy-start.7
  455.3 97.1 %all-to-all-start.6 = ((bf16[4,8,65536]{2,0,1:T(4,128)(2,1)}), bf16[4,8,65536]{2,0,1:T(4,128)(2,1)}, u32[]{:S(2)}, u32[]{:S(2)}) async-start(bf16[4,8,65536]{2,0,1:T(4,128)(2,1)} %copy.90), calls=%async_computation.6 | async-start | bytes 8388608 | tf_op jit(solution)/shard_map/all_to_all | solution.py:108
  552.4 53.2 %all-to-all-start.3 = ((bf16[4,8,65536]{2,1,0:T(8,128)(2,1)}), bf16[4,8,65536]{2,1,0:T(8,128)(2,1)}, u32[]{:S(2)}, u32[]{:S(2)}) async-start(bf16[4,8,65536]{2,1,0:T(8,128)(2,1)} %copy.85), calls=%async_computation.3 | async-start | bytes 8388608 | tf_op jit(solution)/shard_map/all_to_all | solution.py:94
  563.8 47.2 %copy-start.12 = (bf16[1024,384]{1,0:T(8,128)(2,1)S(1)}, bf16[1024,384]{1,0:T(8,128)(2,1)}, u32[]{:S(2)}) copy-start(bf16[1024,384]{1,0:T(8,128)(2,1)} %copy-done.11) | copy-start | bytes 2359300
  605.6 54.8 %all-to-all-start.7 = ((bf16[4,8,65536]{2,1,0:T(8,128)(2,1)}), bf16[4,8,65536]{2,1,0:T(8,128)(2,1)}, u32[]{:S(2)}, u32[]{:S(2)}) async-start(bf16[4,8,65536]{2,1,0:T(8,128)(2,1)} %copy.91), calls=%async_computation.7 | async-start | bytes 8388608 | tf_op jit(solution)/shard_map/all_to_all | solution.py:107
  611.0 5.4 copy-start.3
  611.0 5.4 copy-start.8
  616.4 3.6 copy-start.6
  688.2 8.6 %copy-start.1 = (bf16[1,384,2048]{2,1,0:T(8,128)(2,1)S(1)}, bf16[1,384,2048]{2,1,0:T(8,128)(2,1)}, u32[]{:S(2)}) copy-start(bf16[1,384,2048]{2,1,0:T(8,128)(2,1)} %param.12) | copy-start | bytes 4718596
where the time goes:
time: 709 us; the launch traced here: 697 us
  waiting for transfers between devices  413 us (58%)
  local copies, waits for them, and re-layouts  160 us (23%)
  starting transfers between devices  50.5 us (7%)
  matrix products  41.6 us (6%)
  other arithmetic  30.6 us (4%)
    all_to_all x1, waiting for transfers between devices, local(): lax.all_to_all(qsend, 'dp', split_axis=1, concat_axis=1, tiled=True)  82.8 us
    all_to_all x1, waiting for transfers between devices, local(): lax.all_to_all(pgrad.reshape(n_group, n_data, most * width), 'dp', split_...  82.8 us
    all_to_all x1, waiting for transfers between devices, local(): lax.all_to_all(outv.reshape(n_group, n_data, most * width), 'dp', split_a...  68.9 us
    all_to_all x1, waiting for transfers between devices, local(): lax.all_to_all(xsend, 'dp', split_axis=1, concat_axis=1, tiled=True)  62.6 us
    all_to_all x1, waiting for transfers between devices, local(): lax.all_to_all(lax.all_to_all(xsend, 'dp', split_axis=1, concat_axis=1, t...  41.8 us
    all_to_all x1, waiting for transfers between devices, local(): lax.all_to_all(lax.all_to_all(outv.reshape(n_group, n_data, most * width)...  41.8 us
    all_to_all x1, waiting for transfers between devices, local(): lax.all_to_all(lax.all_to_all(qsend, 'dp', split_axis=1, concat_axis=1, t...  32.8 us
  transfers between devices with their start and end apart: 8, of which 7 were waited for; matrix products, arithmetic and copies ran while one was open for 20% of the time, Pallas kernels for 0%

commit v1 on v0

v1 whole, which is shorter than its diff:
```python
import jax
import jax.numpy as jnp
from jax import lax
from jax.sharding import PartitionSpec as P

AXES = ("dp", "expert")
BF = jnp.bfloat16
F32 = jnp.float32


def dot(a, b):
    return jnp.dot(a, b, preferred_element_type=F32)


def dot_nt(a, b):
    return lax.dot_general(a, b, (((1,), (1,)), ((), ())), preferred_element_type=F32)


def dot_tn(a, b):
    return lax.dot_general(a, b, (((0,), (0,)), ((), ())), preferred_element_type=F32)


def local(tokens, routes, gate_codes, w_gate, w_up, w_down, cot):
    tok_rows, top = routes.shape
    width = tokens.shape[1]
    n_group = lax.axis_size("expert")
    devices = lax.axis_size("dp") * n_group
    experts = devices // 2
    most = max(2, 2 * tok_rows * top // experts)
    slots = experts * most
    same_core = [list(range(core, devices, 2)) for core in range(2)]
    sibling = [(i, i ^ 1) for i in range(n_group)]

    def exchange(rows):
        blocks = rows.reshape(experts, most, width)
        blocks = lax.all_to_all(
            blocks, AXES, split_axis=0, concat_axis=0, axis_index_groups=same_core, tiled=True
        )
        return blocks.reshape(slots, width)

    def swap(rows):
        return lax.ppermute(rows, "expert", sibling)

    expert_ids = routes.reshape(tok_rows * top)
    onehot = (expert_ids[:, None] == jnp.arange(experts, dtype=jnp.int32)[None, :]).astype(
        jnp.int32
    )
    before = jnp.cumsum(onehot, axis=0) - onehot
    position = jnp.sum(before * onehot, axis=1)
    target = (expert_ids * most + position).reshape(tok_rows, top)
    slot_ids = jnp.arange(slots, dtype=jnp.int32)
    place = jnp.zeros((slots, tok_rows), BF)
    code_hi = jnp.zeros((tok_rows, slots), BF)
    code_lo = jnp.zeros((tok_rows, slots), BF)
    gate_slot = jnp.zeros((slots, 1), F32)
    low = gate_codes % 8
    for k in range(top):
        hit = slot_ids[:, None] == target[None, :, k]
        place = place + hit.astype(BF)
        gate_slot = gate_slot + jnp.sum(
            jnp.where(hit, gate_codes[None, :, k].astype(F32), 0.0), axis=1, keepdims=True
        )
        hit_t = target[:, k, None] == slot_ids[None, :]
        code_hi = code_hi + jnp.where(hit_t, (gate_codes - low)[:, k, None], 0).astype(BF)
        code_lo = code_lo + jnp.where(hit_t, low[:, k, None], 0).astype(BF)
    gate_slot = gate_slot / 1024.0

    wg, wu, wd = w_gate[0], w_up[0], w_down[0]
    xmine = exchange(dot(place, tokens).astype(BF))
    qmine = exchange((gate_slot * dot(place, cot)).astype(BF))

    xrows = jnp.concatenate([xmine, swap(xmine)], axis=0)
    act = dot(xrows, wg)
    upv = dot(xrows, wu)
    sig = jax.nn.sigmoid(act)
    silu = act * sig
    hidden = (silu * upv).astype(BF)

    def give_back(rows):
        other = swap(rows[slots:])
        return exchange((rows[:slots].astype(F32) + other.astype(F32)).astype(BF))

    oback = give_back(dot(hidden, wd).astype(BF))

    qrows = jnp.concatenate([qmine, swap(qmine)], axis=0)
    dhid = dot_nt(qrows, wd)
    dact = (dhid * upv * sig * (1.0 + act * (1.0 - sig))).astype(BF)
    dupv = (dhid * silu).astype(BF)
    pback = give_back((dot_nt(dact, wg) + dot_nt(dupv, wu)).astype(BF))

    grad_g = dot_tn(xrows, dact).astype(BF)
    grad_u = dot_tn(xrows, dupv).astype(BF)
    grad_d = dot_tn(hidden, qrows).astype(BF)

    mixed = ((dot(code_hi, oback) + dot(code_lo, oback)) / 1024.0).astype(BF)
    d_tokens = dot_tn(place, pback).astype(BF)
    return (mixed, d_tokens, grad_g[None], grad_u[None], grad_d[None])


def solution(mesh):
    rows = P(AXES, None)
    stack = P(AXES, None, None)
    return jax.shard_map(
        local,
        mesh=mesh,
        in_specs=(rows, rows, rows, stack, stack, stack, rows),
        out_specs=(rows, rows, stack, stack, stack),
        check_vma=False,
    )
```

time: 709 us -> 254 us (0.36); the launches traced: 697 us -> 253 us
  waiting for transfers between devices: 413 us -> 169 us
  local copies, waits for them, and re-layouts: 160 us -> 2.01 us
  starting transfers between devices: 50.5 us -> 23.5 us
  other arithmetic: 30.6 us -> 5.94 us
  matrix products: 41.6 us -> 52.2 us
    all_to_all x8 -> x4, waiting for transfers between devices: 413 us -> 161 us  [exchange(): lax.all_to_all(blocks, AXES, split_axis=0, concat_axis=0, axis_index_grou...]
    reshape x16 -> x0, local copies, waits for them, and re-layouts: 78.5 us -> none  [the longest x2 13 us: local(): xsend = tok_pad[row_token].reshape(n_group, n_data, most * width)]
    gather x4 -> x0, local copies, waits for them, and re-layouts: 28.3 us -> none  [the longest x1 8.24 us: local(): pback.reshape(total, width)[back_idx].astype(jnp.float32)]
    all_to_all x8 -> x4, starting transfers between devices: 50.5 us -> 22.6 us  [exchange(): lax.all_to_all(blocks, AXES, split_axis=0, concat_axis=0, axis_index_grou...]
    reduce_sum x4 -> x1, other arithmetic: 27.6 us -> 0.22 us  [local(): jnp.sum(jnp.where(hit, gate_codes[None, :, k].astype(F32), 0.0), axis=1,...]
    all_to_all x4 -> x0, local copies, waits for them, and re-layouts: 25.7 us -> none  [the longest x1 6.46 us: local(): lax.all_to_all(outv.reshape(n_group, n_data, most * width), 'dp', split_a...]
    convert_element_type x2 -> x0, local copies, waits for them, and re-layouts: 11.1 us -> none  [the longest x1 5.62 us: local(): oback.reshape(total, width)[back_idx].astype(jnp.float32)]
    dot_general x9 -> x14, matrix products: 41.6 us -> 52.2 us  [the longest x7 21.7 us: dot(): return jnp.dot(a, b, preferred_element_type=F32)]
  transfers between devices with their start and end apart: 8 -> 8, of which waited for: 7 -> 6; matrix products, arithmetic and copies ran while one was open for 20% -> 14% of each run, Pallas kernels for 0% -> 0%
where the time goes in v1:
time: 254 us; the launch traced here: 253 us
  waiting for transfers between devices  169 us (67%)
  matrix products  52.2 us (21%)
  starting transfers between devices  23.5 us (9%)
  other arithmetic  5.94 us (2%)
    all_to_all x4, waiting for transfers between devices, exchange(): lax.all_to_all(blocks, AXES, split_axis=0, concat_axis=0, axis_index_grou...  161 us
    all_to_all x4, starting transfers between devices, exchange(): lax.all_to_all(blocks, AXES, split_axis=0, concat_axis=0, axis_index_grou...  22.6 us
    dot_general x7, matrix products, dot(): return jnp.dot(a, b, preferred_element_type=F32)  21.7 us
    dot_general x4, matrix products, dot_tn(): lax.dot_general(a, b, (((0,), (0,)), ((), ())), preferred_element_type=F32)  19.7 us
    dot_general x3, matrix products, dot_nt(): lax.dot_general(a, b, (((1,), (1,)), ((), ())), preferred_element_type=F32)  10.9 us
    ppermute x4, waiting for transfers between devices, swap(): return lax.ppermute(rows, 'expert', sibling)  7.58 us
  transfers between devices with their start and end apart: 8, of which 6 were waited for; matrix products, arithmetic and copies ran while one was open for 14% of the time, Pallas kernels for 0%

profile of v1, /device:TPU:12, one launch (start us, length us, event | category | flops | bytes accessed | tf_op | source)
XLA Modules:
  0.0 253.3 jit_solution(7586506164066921487)
XLA Ops:
  0.6 0.0 copy-start
  0.6 0.9 copy.27
  1.6 0.1 eq.87
  1.7 0.1 eq.83
  1.8 0.6 reduce-window.6
  2.4 0.2 slice_reduce_fusion
  2.7 0.1 fusion.45
  2.8 0.1 reduce_sum.30
  2.9 0.1 copy.30
  3.0 0.7 multiply_add_fusion
  3.7 3.1 %convolution_convert_fusion.1 = bf16[512,2048]{1,0:T(8,128)(2,1)} fusion(bf16[128,2048]{1,0:T(8,128)(2,1)} %param.7, s32[128]{0:T(128)S(1)} %get-tuple-element.17, s32[128]{0:T(128)S(1)} %get-tuple-element.16), kind=kOutput, calls=%fused_computation.7 | convolution fusion | flops 270008320 | bytes 2622464 | tf_op jit(solution)/shard_map/dot_general | solution.py:12
  6.7 0.0 copy-start.8
  6.7 7.3 %all-to-all-start = ((bf16[16,32,2048]{2,1,0:T(8,128)(2,1)}), bf16[16,32,2048]{2,1,0:T(8,128)(2,1)}, u32[]{:S(2)}, u32[]{:S(2)}) async-start(bf16[16,32,2048]{2,1,0:T(8,128)(2,1)} %bitcast.79), calls=%async_computation | async-start | bytes 4194304 | tf_op jit(solution)/shard_map/all_to_all | solution.py:36
  14.0 0.0 copy-done.8
  14.1 0.2 select_reduce_fusion
  14.3 0.0 copy-done.7
  14.3 2.0 multiply_convert_fusion
  16.4 45.9 %all-to-all-done = bf16[16,32,2048]{2,1,0:T(8,128)(2,1)} async-done(((bf16[16,32,2048]{2,1,0:T(8,128)(2,1)}), bf16[16,32,2048]{2,1,0:T(8,128)(2,1)}, u32[]{:S(2)}, u32[]{:S(2)}) %all-to-all-start) | async-done | bytes 2097184 | tf_op jit(solution)/shard_map/all_to_all | solution.py:36
  62.3 0.0 copy-start.2
  62.3 5.0 %all-to-all-start.2 = ((bf16[16,32,2048]{2,1,0:T(8,128)(2,1)}), bf16[16,32,2048]{2,1,0:T(8,128)(2,1)}, u32[]{:S(2)}, u32[]{:S(2)}) async-start(bf16[16,32,2048]{2,1,0:T(8,128)(2,1)} %bitcast.80), calls=%async_computation.2 | async-start | bytes 4194304 | tf_op jit(solution)/shard_map/all_to_all | solution.py:36
  67.3 0.1 collective-permute-start
  67.4 47.7 %all-to-all-done.2 = bf16[16,32,2048]{2,1,0:T(8,128)(2,1)} async-done(((bf16[16,32,2048]{2,1,0:T(8,128)(2,1)}), bf16[16,32,2048]{2,1,0:T(8,128)(2,1)}, u32[]{:S(2)}, u32[]{:S(2)}) %all-to-all-start.2) | async-done | bytes 2097184 | tf_op jit(solution)/shard_map/all_to_all | solution.py:36
  115.1 0.0 copy-start.1
  115.1 0.0 collective-permute-start.2
  115.1 0.0 collective-permute-done
  115.1 0.0 copy-done.2
  115.1 4.7 %fusion.9 = f32[1024,384]{1,0:T(8,128)S(1)} fusion(bf16[1,2048,384]{2,1,0:T(8,128)(2,1)S(1)} %copy-done.2, bf16[512,2048]{1,0:T(8,128)(2,1)} %collective-permute-done, bf16[512,2048]{1,0:T(8,128)(2,1)} %bitcast.6), kind=kOutput, calls=%fused_computation.22 | convolution fusion | flops 1619001344 | bytes 7340032 | tf_op jit(solution)/shard_map/dot_general | solution.py:12
  119.8 0.0 copy-done.1
  119.8 4.5 %fusion.13 = f32[1024,384]{1,0:T(8,128)S(1)} fusion(bf16[1,2048,384]{2,1,0:T(8,128)(2,1)S(1)} %copy-done.1, bf16[512,2048]{1,0:T(8,128)(2,1)} %collective-permute-done, bf16[512,2048]{1,0:T(8,128)(2,1)} %bitcast.6), kind=kOutput, calls=%fused_computation.26 | convolution fusion | flops 1619001344 | bytes 7340032 | tf_op jit(solution)/shard_map/dot_general | solution.py:12
  124.3 0.0 collective-permute-done.2
  124.3 0.0 copy-done
  124.4 0.0 copy-start.9
  124.4 6.1 %multiply_convert_fusion.1 = (bf16[1024,384]{1,0:T(8,128)(2,1)S(1)}, bf16[1024,384]{1,0:T(8,128)(2,1)S(1)}, bf16[1024,384]{1,0:T(8,128)(2,1)}) fusion(f32[1024,384]{1,0:T(8,128)S(1)} %fusion.13, f32[1024,384]{1,0:T(8,128)S(1)} %fusion.9, bf16[1,384,2048]{2,1,0:T(8,128)(2,1)S(1)} %copy-done, bf16[512,2048]{1,0:T(8,128)(2,1)S(1)} %collective-permute-done.2, ...), kind=kOutput, calls=%fused_computation.28 | convolution fusion | flops 1624899584 | bytes 11272192 | tf_op jit(solution)/shard_map/dot_general | solution.py:16
  130.5 0.0 copy-done.9
  130.5 0.0 copy-start.3
  130.5 0.0 copy-start.5
  130.5 2.4 fusion.11
  132.8 0.0 copy-done.3
  132.9 0.0 copy-done.5
  132.9 2.4 add_convert_fusion
  135.3 0.2 slice.62
  135.5 0.4 collective-permute-start.3
  135.9 3.8 %collective-permute-done.3 = bf16[512,2048]{1,0:T(8,128)(2,1)S(1)} collective-permute-done((bf16[512,2048]{1,0:T(8,128)(2,1)S(1)}, bf16[512,2048]{1,0:T(8,128)(2,1)S(1)}, u32[]{:S(2)}, u32[]{:S(2)}) %collective-permute-start.3) | collective-permute-done | bytes 2097184 | tf_op jit(solution)/shard_map/ppermute | solution.py:42
  139.7 2.1 add_convert_fusion.1
  141.8 0.0 copy-start.10
  141.8 4.7 %all-to-all-start.3 = ((bf16[16,32,2048]{2,1,0:T(8,128)(2,1)}), bf16[16,32,2048]{2,1,0:T(8,128)(2,1)}, u32[]{:S(2)}, u32[]{:S(2)}) async-start(bf16[16,32,2048]{2,1,0:T(8,128)(2,1)} %bitcast.78), calls=%async_computation.3 | async-start | bytes 4194304 | tf_op jit(solution)/shard_map/all_to_all | solution.py:36
  146.5 0.0 copy-done.10
  146.6 2.3 convolution_convert_fusion
  148.9 0.1 slice.60
  149.0 0.4 collective-permute-start.1
  149.5 3.8 %collective-permute-done.1 = bf16[512,2048]{1,0:T(8,128)(2,1)S(1)} collective-permute-done((bf16[512,2048]{1,0:T(8,128)(2,1)S(1)}, bf16[512,2048]{1,0:T(8,128)(2,1)S(1)}, u32[]{:S(2)}, u32[]{:S(2)}) %collective-permute-start.1) | collective-permute-done | bytes 2097184 | tf_op jit(solution)/shard_map/ppermute | solution.py:42
  153.3 2.2 add_convert_fusion.2
  155.4 39.4 %all-to-all-done.3 = bf16[16,32,2048]{2,1,0:T(8,128)(2,1)} async-done(((bf16[16,32,2048]{2,1,0:T(8,128)(2,1)}), bf16[16,32,2048]{2,1,0:T(8,128)(2,1)}, u32[]{:S(2)}, u32[]{:S(2)}) %all-to-all-start.3) | async-done | bytes 2097184 | tf_op jit(solution)/shard_map/all_to_all | solution.py:36
  194.8 5.5 %all-to-all-start.1 = ((bf16[16,32,2048]{2,1,0:T(8,128)(2,1)}), bf16[16,32,2048]{2,1,0:T(8,128)(2,1)}, u32[]{:S(2)}, u32[]{:S(2)}) async-start(bf16[16,32,2048]{2,1,0:T(8,128)(2,1)} %bitcast.77), calls=%async_computation.1 | async-start | bytes 4194304 | tf_op jit(solution)/shard_map/all_to_all | solution.py:36
  200.4 0.0 copy-start.6
  200.4 5.3 %fusion.3 = bf16[1,384,2048]{2,1,0:T(8,128)(2,1)} fusion(bf16[1024,384]{1,0:T(8,128)(2,1)S(1)} %copy-done.10, bf16[512,2048]{1,0:T(8,128)(2,1)} %copy-done.9, bf16[512,2048]{1,0:T(8,128)(2,1)} %bitcast.17), kind=kOutput, calls=%fused_computation.14 | convolution fusion | flops 1619787776 | bytes 6553600 | tf_op jit(solution)/shard_map/dot_general | solution.py:20
  205.7 0.0 copy-done.6
  205.7 5.8 %fusion.2 = bf16[1,2048,384]{2,1,0:T(8,128)(2,1)} fusion(bf16[1024,384]{1,0:T(8,128)(2,1)S(1)} %copy-done.6, bf16[512,2048]{1,0:T(8,128)(2,1)} %collective-permute-done, bf16[512,2048]{1,0:T(8,128)(2,1)} %bitcast.6), kind=kOutput, calls=%fused_computation.13 | convolution fusion | flops 1619787776 | bytes 6553600 | tf_op jit(solution)/shard_map/dot_general | solution.py:20
  211.5 0.0 copy-done.4
  211.5 5.8 %fusion.1 = bf16[1,2048,384]{2,1,0:T(8,128)(2,1)} fusion(bf16[1024,384]{1,0:T(8,128)(2,1)S(1)} %copy-done.4, bf16[512,2048]{1,0:T(8,128)(2,1)} %collective-permute-done, bf16[512,2048]{1,0:T(8,128)(2,1)} %bitcast.6), kind=kOutput, calls=%fused_computation.12 | convolution fusion | flops 1619787776 | bytes 6553600 | tf_op jit(solution)/shard_map/dot_general | solution.py:20
  217.3 2.9 %convolution_convert_fusion.5 = bf16[128,2048]{1,0:T(8,128)(2,1)} fusion(bf16[512,2048]{1,0:T(8,128)(2,1)} %bitcast.19, s32[128]{0:T(128)S(1)} %get-tuple-element.17, s32[128]{0:T(128)S(1)} %get-tuple-element.16), kind=kOutput, calls=%fused_computation.18 | convolution fusion | flops 269221888 | bytes 2622464 | tf_op jit(solution)/shard_map/dot_general | solution.py:20
  220.1 28.1 %all-to-all-done.1 = bf16[16,32,2048]{2,1,0:T(8,128)(2,1)} async-done(((bf16[16,32,2048]{2,1,0:T(8,128)(2,1)}), bf16[16,32,2048]{2,1,0:T(8,128)(2,1)}, u32[]{:S(2)}, u32[]{:S(2)}) %all-to-all-start.1) | async-done | bytes 2097184 | tf_op jit(solution)/shard_map/all_to_all | solution.py:36
  248.3 2.1 fusion.25
  250.4 2.9 %fusion.5 = bf16[128,2048]{1,0:T(8,128)(2,1)} fusion(f32[128,2048]{1,0:T(8,128)S(1)} %fusion.25, bf16[512,2048]{1,0:T(8,128)(2,1)} %bitcast.11, s32[128]{0:T(128)S(1)} %get-tuple-element.20, s32[128]{0:T(128)S(1)} %get-tuple-element.17, s32[128]{0:T(128)S(1)} %get-tuple-element.21, s32[128]{0:T(128)S(1)} %get-tuple-element.16), kind=kOutput, calls=%fused_computation.17 | convolution fusion | flops 269877248 | bytes 3672064 | tf_op jit(solution)/shard_map/dot_general | solution.py:12
  (10 shorter events, 0.1 us)
Async XLA Ops:
  0.6 123.7 %copy-start = (bf16[1,384,2048]{2,1,0:T(8,128)(2,1)S(1)}, bf16[1,384,2048]{2,1,0:T(8,128)(2,1)}, u32[]{:S(2)}) copy-start(bf16[1,384,2048]{2,1,0:T(8,128)(2,1)} %param.12) | copy-start | bytes 4718596
  6.7 7.3 %copy-start.8 = (s32[128,2]{0,1:T(2,128)S(1)}, s32[128,2]{0,1:T(2,128)}, u32[]{:S(2)}) copy-start(s32[128,2]{0,1:T(2,128)} %param.9) | copy-start | bytes 3076
  6.7 7.6 %copy-start.7 = (bf16[128,2048]{1,0:T(8,128)(2,1)S(1)}, bf16[128,2048]{1,0:T(8,128)(2,1)}, u32[]{:S(2)}) copy-start(bf16[128,2048]{1,0:T(8,128)(2,1)} %param.13) | copy-start | bytes 1572868
  6.7 55.5 %all-to-all-start = ((bf16[16,32,2048]{2,1,0:T(8,128)(2,1)}), bf16[16,32,2048]{2,1,0:T(8,128)(2,1)}, u32[]{:S(2)}, u32[]{:S(2)}) async-start(bf16[16,32,2048]{2,1,0:T(8,128)(2,1)} %bitcast.79), calls=%async_computation | async-start | bytes 4194304 | tf_op jit(solution)/shard_map/all_to_all | solution.py:36
  62.3 52.8 %copy-start.2 = (bf16[1,2048,384]{2,1,0:T(8,128)(2,1)S(1)}, bf16[1,2048,384]{2,1,0:T(8,128)(2,1)}, u32[]{:S(2)}) copy-start(bf16[1,2048,384]{2,1,0:T(8,128)(2,1)} %param.11) | copy-start | bytes 4718596
  62.3 52.8 %all-to-all-start.2 = ((bf16[16,32,2048]{2,1,0:T(8,128)(2,1)}), bf16[16,32,2048]{2,1,0:T(8,128)(2,1)}, u32[]{:S(2)}, u32[]{:S(2)}) async-start(bf16[16,32,2048]{2,1,0:T(8,128)(2,1)} %bitcast.80), calls=%async_computation.2 | async-start | bytes 4194304 | tf_op jit(solution)/shard_map/all_to_all | solution.py:36
  67.3 47.8 %collective-permute-start = (bf16[512,2048]{1,0:T(8,128)(2,1)}, bf16[512,2048]{1,0:T(8,128)(2,1)}, u32[]{:S(2)}, u32[]{:S(2)}) collective-permute-start(bf16[512,2048]{1,0:T(8,128)(2,1)} %bitcast.6), channel_id=1, source_target_pairs={{0,1},{1,0},{2,3},{3,2},{4,5},{5,4},{6,7},{7,6},{8,9},{9,8},{10,11... | collective-permute-start | bytes 6291464 | tf_op jit(solution)/shard_map/ppermute | solution.py:42
  115.1 4.7 %copy-start.1 = (bf16[1,2048,384]{2,1,0:T(8,128)(2,1)S(1)}, bf16[1,2048,384]{2,1,0:T(8,128)(2,1)}, u32[]{:S(2)}) copy-start(bf16[1,2048,384]{2,1,0:T(8,128)(2,1)} %param.10) | copy-start | bytes 4718596
  115.1 9.2 %collective-permute-start.2 = (bf16[512,2048]{1,0:T(8,128)(2,1)}, bf16[512,2048]{1,0:T(8,128)(2,1)S(1)}, u32[]{:S(2)}, u32[]{:S(2)}) collective-permute-start(bf16[512,2048]{1,0:T(8,128)(2,1)} %bitcast.17), channel_id=1, source_target_pairs={{0,1},{1,0},{2,3},{3,2},{4,5},{5,4},{6,7},{7,6},{8,9},{9,8},{10,11... | collective-permute-start | bytes 6291464 | tf_op jit(solution)/shard_map/ppermute | solution.py:42
  124.4 6.1 %copy-start.9 = (bf16[512,2048]{1,0:T(8,128)(2,1)}, bf16[512,2048]{1,0:T(8,128)(2,1)S(1)}, u32[]{:S(2)}) copy-start(bf16[512,2048]{1,0:T(8,128)(2,1)S(1)} %collective-permute-done.2) | copy-start | bytes 6291460
  130.5 2.4 copy-start.3
  130.5 2.4 copy-start.5
  135.5 4.2 %collective-permute-start.3 = (bf16[512,2048]{1,0:T(8,128)(2,1)S(1)}, bf16[512,2048]{1,0:T(8,128)(2,1)S(1)}, u32[]{:S(2)}, u32[]{:S(2)}) collective-permute-start(bf16[512,2048]{1,0:T(8,128)(2,1)S(1)} %slice.62), channel_id=1, source_target_pairs={{0,1},{1,0},{2,3},{3,2},{4,5},{5,4},{6,7},{7,6},{8,9},{9,8},{10,11... | collective-permute-start | bytes 6291464 | tf_op jit(solution)/shard_map/ppermute | solution.py:42
  141.8 4.7 %copy-start.10 = (bf16[1024,384]{1,0:T(8,128)(2,1)S(1)}, bf16[1024,384]{1,0:T(8,128)(2,1)}, u32[]{:S(2)}) copy-start(bf16[1024,384]{1,0:T(8,128)(2,1)} %get-tuple-element.9) | copy-start | bytes 2359300
  141.8 53.0 %all-to-all-start.3 = ((bf16[16,32,2048]{2,1,0:T(8,128)(2,1)}), bf16[16,32,2048]{2,1,0:T(8,128)(2,1)}, u32[]{:S(2)}, u32[]{:S(2)}) async-start(bf16[16,32,2048]{2,1,0:T(8,128)(2,1)} %bitcast.78), calls=%async_computation.3 | async-start | bytes 4194304 | tf_op jit(solution)/shard_map/all_to_all | solution.py:36
  149.0 4.2 %collective-permute-start.1 = (bf16[512,2048]{1,0:T(8,128)(2,1)S(1)}, bf16[512,2048]{1,0:T(8,128)(2,1)S(1)}, u32[]{:S(2)}, u32[]{:S(2)}) collective-permute-start(bf16[512,2048]{1,0:T(8,128)(2,1)S(1)} %slice.60), channel_id=1, source_target_pairs={{0,1},{1,0},{2,3},{3,2},{4,5},{5,4},{6,7},{7,6},{8,9},{9,8},{10,11... | collective-permute-start | bytes 6291464 | tf_op jit(solution)/shard_map/ppermute | solution.py:42
  194.8 53.4 %all-to-all-start.1 = ((bf16[16,32,2048]{2,1,0:T(8,128)(2,1)}), bf16[16,32,2048]{2,1,0:T(8,128)(2,1)}, u32[]{:S(2)}, u32[]{:S(2)}) async-start(bf16[16,32,2048]{2,1,0:T(8,128)(2,1)} %bitcast.77), calls=%async_computation.1 | async-start | bytes 4194304 | tf_op jit(solution)/shard_map/all_to_all | solution.py:36
  200.4 5.3 %copy-start.6 = (bf16[1024,384]{1,0:T(8,128)(2,1)S(1)}, bf16[1024,384]{1,0:T(8,128)(2,1)}, u32[]{:S(2)}) copy-start(bf16[1024,384]{1,0:T(8,128)(2,1)} %copy-done.5) | copy-start | bytes 2359300
  205.7 5.8 %copy-start.4 = (bf16[1024,384]{1,0:T(8,128)(2,1)S(1)}, bf16[1024,384]{1,0:T(8,128)(2,1)}, u32[]{:S(2)}) copy-start(bf16[1024,384]{1,0:T(8,128)(2,1)} %copy-done.3) | copy-start | bytes 2359300
